TPU v7x, 128 devices: a whole 4x4x4 slice. The times are simulated.
128 devices in a mesh: row: 16 (over x, y), col: 8 (over z, core).
Axes of the slice: x: 4, y: 4, z: 4, core: 2. Of those that a mesh axis runs over, the one named last changes fastest.
Arguments:
- source_points: bfloat16 [65536, 1024], P('row'), may hold values from -8 to 8
- target_points: bfloat16 [32768, 1024], P('col', 'row'), may hold values from -8 to 8
- source_mass: float32 [65536], P('row'), may hold values from 0.25 to 4
- target_mass: float32 [32768], P('col'), may hold values from 0.25 to 4
- tile_index: int32 [256, 16], P('row', 'col'), may hold values from 0 to 15, as said below
- tile_count: int32 [256, 8], P('row', 'col'), may hold values from 1 to 2, as said below
Outputs:
- source_potential: float32 [65536], P('row')
- target_potential: float32 [32768], P('col')
Inputs may be any that keep to these rules, and one draw needn't show every extreme that they name: `tile_index`: within the 2 slots of one source tile and one index of col the target tiles are distinct; every target tile is named by a live slot of some source tile. `tile_count`: each index of row holds, for every index of col, a source tile with all 2 slots live.
All inputs are finite; a program needn't handle non-finite values.
Results may differ from a plain program's by a relative error of at most 0.0003.
Values may be sent and summed in bfloat16 or wider, within the bound.
A program may use at most 128 MiB of HBM per device.

v0:
```python
import math
import jax
import jax.numpy as jnp
from jax import lax
from jax.sharding import PartitionSpec as P

TILE = 256
ITERS = 3
masked_score = -1e30


def cost_terms(piece, source_points, tile_index):
    width = piece.shape[1]
    source_tiles = source_points.reshape(-1, TILE, width)
    target_tiles = piece.reshape(-1, TILE, width)
    chosen = target_tiles[tile_index]
    return jnp.einsum("rad,rkbd->rkab", source_tiles, chosen, preferred_element_type=jnp.float32)


def on_device(source_points, target_points, source_mass, target_mass, tile_index, tile_count):
    tiles_per_row = source_points.shape[0] // TILE
    col_tiles = target_points.shape[0] // TILE
    slot_count = tile_index.shape[1]
    scale = 1.0 / math.sqrt(source_points.shape[1])
    live = jnp.arange(slot_count)[None, :] < tile_count
    onehot = (tile_index[:, :, None] == jnp.arange(col_tiles)[None, None, :]) & live[:, :, None]
    log_source = jnp.log(source_mass).reshape(tiles_per_row, TILE)
    log_target = jnp.log(target_mass).reshape(col_tiles, TILE)
    target_pot = jnp.zeros((col_tiles, TILE), jnp.float32)
    source_pot = jnp.zeros((tiles_per_row, TILE), jnp.float32)
    for iteration in range(ITERS):
        cost = (
            cost_terms(
                lax.all_gather(target_points, "row", axis=1, tiled=True), source_points, tile_index
            )
            * scale
        )
        scores = cost + target_pot[tile_index][:, :, None, :]
        scores = jnp.where(live[:, :, None, None], scores, masked_score)
        row_top = jnp.max(scores, axis=(1, 3))
        highest = lax.pmax(row_top, "col")
        local_sum = jnp.sum(jnp.exp(scores - highest[:, None, :, None]), axis=(1, 3))
        total = lax.psum(local_sum, "col")
        source_pot = log_source - highest - jnp.log(total)
        columns = cost + source_pot[:, None, :, None]
        columns = jnp.where(live[:, :, None, None], columns, masked_score)
        slot_top = jnp.max(columns, axis=2)
        local_top = jnp.max(
            jnp.where(onehot[..., None], slot_top[:, :, None, :], masked_score), axis=(0, 1)
        )
        col_high = lax.pmax(local_top, "row")
        slot_ref = col_high[tile_index]
        sums = jnp.sum(jnp.exp(columns - slot_ref[:, :, None, :]), axis=2)
        col_sum = jnp.sum(jnp.where(onehot[..., None], sums[:, :, None, :], 0.0), axis=(0, 1))
        col_total = lax.psum(col_sum, "row")
        target_pot = log_target - col_high - jnp.log(col_total)
    return (source_pot.reshape(-1), target_pot.reshape(-1))


def solution(mesh):
    placed = (P("row", None), P("col", "row"), P("row"), P("col"), P("row", "col"), P("row", "col"))
    return jax.shard_map(
        on_device, mesh=mesh, in_specs=placed, out_specs=(P("row"), P("col")), check_vma=False
    )
```

profile of v0, /device:TPU:0, one launch (start us, length us, event | category | flops | bytes accessed | tf_op | source)
XLA Modules:
  0.0 747.5 jit_solution(9227641684370280702)
XLA Ops:
  7.9 0.8 copy.16
  8.7 0.7 compare_select_fusion
  10.2 0.7 log.24
  10.9 0.7 log.25
  11.6 0.7 iota_compare_fusion
  12.5 70.8 %all-gather.2.cloned.1.call-done = bf16[4096,1024]{0,1:T(8,128)(2,1)} async-done(((bf16[4096,64]{0,1:T(8,128)(2,1)}), bf16[4096,1024]{0,1:T(8,128)(2,1)}) %all-gather.2.cloned.1.call-update) | async-done | bytes 8388624 | tf_op jit(solution)/shard_map/all_gather | solution.py:34
  83.2 12.0 %copy.14 = bf16[4096,1024]{1,0:T(8,128)(2,1)} copy(bf16[4096,1024]{0,1:T(8,128)(2,1)} %all-gather.2.cloned.1.call-done) | data formatting | bytes 16777216 | tf_op jit(solution)/shard_map/all_gather | solution.py:34
  95.2 10.6 %gather_fusion = bf16[32,256,1024]{2,1,0:T(8,128)(2,1)} fusion(bf16[16,256,1024]{2,1,0:T(8,128)(2,1)} %bitcast.57, s32[1024]{0:T(1024)S(1)} %pad_clamp_fusion), kind=kCustom, calls=%fused_computation | custom fusion | bytes 33554560 | tf_op jit(solution)/shard_map/gather | solution.py:16
  105.8 13.5 %bitcast_reduce_fusion.5 = (f32[16,256]{1,0:T(8,128)S(1)}, f32[16,2,256,256]{3,2,1,0:T(8,128)}) fusion(f32[16,2,256]{2,1,0:T(2,128)S(1)} %reshape.108, pred[16,2]{1,0:T(8,128)(4,1)S(1)} %iota_compare_fusion, bf16[16,2,256,1024]{3,2,1,0:T(8,128)(2,1)} %bitcast.58, bf16[16,256,1024,1]{2,1,3,0:T(8,128)(2,1)} %bitcast.63), kind=kOutput, calls=%fused_computation.28 | convolution fusion | flops 4303351808 | bytes 33603616 | tf_op jit(solution)/shard_map/rad,rkbd->rkab/dot_general | solution.py:17
  119.3 25.8 %pmax.42 = f32[16,256]{1,0:T(8,128)S(1)} all-reduce(f32[16,256]{1,0:T(8,128)S(1)} %get-tuple-element.2), channel_id=1, replica_groups=mesh['row'=16,'col'=8] {'col'}, use_global_device_ids=true, to_apply=%region_1.2 | all-reduce | flops 4096 | bytes 32768 | tf_op jit(solution)/shard_map/pmax | solution.py:41
  145.1 4.6 fusion.11
  149.8 23.6 %psum.42 = f32[16,256]{1,0:T(8,128)S(1)} all-reduce(f32[16,256]{1,0:T(8,128)S(1)} %fusion.11), channel_id=1, replica_groups=mesh['row'=16,'col'=8] {'col'}, use_global_device_ids=true, to_apply=%region_3.4 | all-reduce | flops 4096 | bytes 32768 | tf_op jit(solution)/shard_map/psum | solution.py:43
  173.3 4.7 bitcast_reduce_fusion.4
  178.1 72.4 %pmax.43 = f32[16,256]{1,0:T(8,128)S(1)} all-reduce(f32[16,256]{1,0:T(8,128)S(1)} %select_reduce_fusion.5), channel_id=1, replica_groups=mesh['row'=16,'col'=8] {'row'}, use_global_device_ids=true, to_apply=%region_6.7 | all-reduce | flops 4096 | bytes 32768 | tf_op jit(solution)/shard_map/pmax | solution.py:51
  251.1 5.1 fusion.9
  256.4 69.5 %psum.43 = f32[16,256]{1,0:T(8,128)S(1)} all-reduce(f32[16,256]{1,0:T(8,128)S(1)} %select_reduce_fusion.4), channel_id=1, replica_groups=mesh['row'=16,'col'=8] {'row'}, use_global_device_ids=true, to_apply=%region_9.10 | all-reduce | flops 4096 | bytes 32768 | tf_op jit(solution)/shard_map/psum | solution.py:55
  326.6 4.4 bitcast_reduce_fusion.3
  331.0 23.7 %pmax.44 = f32[16,256]{1,0:T(8,128)S(1)} all-reduce(f32[16,256]{1,0:T(8,128)S(1)} %bitcast_reduce_fusion.3), channel_id=1, replica_groups=mesh['row'=16,'col'=8] {'col'}, use_global_device_ids=true, to_apply=%region_11.12 | all-reduce | flops 4096 | bytes 32768 | tf_op jit(solution)/shard_map/pmax | solution.py:41
  354.8 4.6 fusion.7
  359.4 23.6 %psum.44 = f32[16,256]{1,0:T(8,128)S(1)} all-reduce(f32[16,256]{1,0:T(8,128)S(1)} %fusion.7), channel_id=1, replica_groups=mesh['row'=16,'col'=8] {'col'}, use_global_device_ids=true, to_apply=%region_13.14 | all-reduce | flops 4096 | bytes 32768 | tf_op jit(solution)/shard_map/psum | solution.py:43
  383.0 4.7 bitcast_reduce_fusion.2
  387.8 69.5 %pmax.45 = f32[16,256]{1,0:T(8,128)S(1)} all-reduce(f32[16,256]{1,0:T(8,128)S(1)} %select_reduce_fusion.3), channel_id=1, replica_groups=mesh['row'=16,'col'=8] {'row'}, use_global_device_ids=true, to_apply=%region_16.17 | all-reduce | flops 4096 | bytes 32768 | tf_op jit(solution)/shard_map/pmax | solution.py:51
  458.0 5.1 fusion.5
  463.2 69.5 %psum.45 = f32[16,256]{1,0:T(8,128)S(1)} all-reduce(f32[16,256]{1,0:T(8,128)S(1)} %select_reduce_fusion.2), channel_id=1, replica_groups=mesh['row'=16,'col'=8] {'row'}, use_global_device_ids=true, to_apply=%region_19.20 | all-reduce | flops 4096 | bytes 32768 | tf_op jit(solution)/shard_map/psum | solution.py:55
  533.4 4.4 bitcast_reduce_fusion.1
  537.8 23.6 %pmax.46 = f32[16,256]{1,0:T(8,128)S(1)} all-reduce(f32[16,256]{1,0:T(8,128)S(1)} %bitcast_reduce_fusion.1), channel_id=1, replica_groups=mesh['row'=16,'col'=8] {'col'}, use_global_device_ids=true, to_apply=%region_21.22 | all-reduce | flops 4096 | bytes 32768 | tf_op jit(solution)/shard_map/pmax | solution.py:41
  561.4 4.6 fusion.3
  566.0 23.6 %psum.46 = f32[16,256]{1,0:T(8,128)S(1)} all-reduce(f32[16,256]{1,0:T(8,128)S(1)} %fusion.3), channel_id=1, replica_groups=mesh['row'=16,'col'=8] {'col'}, use_global_device_ids=true, to_apply=%region_23.24 | all-reduce | flops 4096 | bytes 32768 | tf_op jit(solution)/shard_map/psum | solution.py:43
  589.6 4.7 bitcast_reduce_fusion
  594.4 69.5 %pmax.47 = f32[16,256]{1,0:T(8,128)S(1)} all-reduce(f32[16,256]{1,0:T(8,128)S(1)} %select_reduce_fusion.1), channel_id=1, replica_groups=mesh['row'=16,'col'=8] {'row'}, use_global_device_ids=true, to_apply=%region_26.27 | all-reduce | flops 4096 | bytes 32768 | tf_op jit(solution)/shard_map/pmax | solution.py:51
  664.6 5.1 fusion.1
  669.8 69.5 %psum.47 = f32[16,256]{1,0:T(8,128)S(1)} all-reduce(f32[16,256]{1,0:T(8,128)S(1)} %select_reduce_fusion), channel_id=1, replica_groups=mesh['row'=16,'col'=8] {'row'}, use_global_device_ids=true, to_apply=%region_29.30 | all-reduce | flops 4096 | bytes 32768 | tf_op jit(solution)/shard_map/psum | solution.py:55
  (35 shorter events, 6.9 us)
Async XLA Ops:
  7.2 76.1 %all-gather.2.cloned.1.call-start = ((), (), s32[]{:S(2)}) async-start(), calls=%async_computation | async-start | bytes 8912896 | tf_op jit(solution)/shard_map/all_gather | solution.py:34
Sparse Core Ops, SparseCore 0:
  10.1 73.0 all-gather.1
where the time goes:
time: 748 us; the launch traced here: 747 us
  blocking collectives  564 us (75%)
  waiting for transfers between devices  71.4 us (10%)
  other arithmetic  54.5 us (7%)
  local copies, waits for them, and re-layouts  30 us (4%)
  between operations  14.3 us (2%)
  matrix products  13.5 us (2%)
    pmax x3, blocking collectives, on_device(): col_high = lax.pmax(local_top, 'row')  211 us
    psum x3, blocking collectives, on_device(): col_total = lax.psum(col_sum, 'row')  209 us
    pmax x3, blocking collectives, on_device(): highest = lax.pmax(row_top, 'col')  73.1 us
    all_gather x1, waiting for transfers between devices, on_device(): lax.all_gather(target_points, 'row', axis=1, tiled=True)  70.8 us
    psum x3, blocking collectives, on_device(): total = lax.psum(local_sum, 'col')  70.7 us
    reduce_sum x3, other arithmetic, on_device(): sums = jnp.sum(jnp.exp(columns - slot_ref[:, :, None, :]), axis=2)  15.4 us
  transfers between devices with their start and end apart: 1, of which 1 were waited for; matrix products, arithmetic and copies ran while one was open for 1% of the time, Pallas kernels for 0%

commit v1 on v0

--- a/solution.py
+++ b/solution.py
@@ -40,7 +40,7 @@
         row_top = jnp.max(scores, axis=(1, 3))
         highest = lax.pmax(row_top, "col")
         local_sum = jnp.sum(jnp.exp(scores - highest[:, None, :, None]), axis=(1, 3))
-        total = lax.psum(local_sum, "col")
+        total = jnp.sum(lax.all_gather(local_sum, "col"), axis=0)
         source_pot = log_source - highest - jnp.log(total)
         columns = cost + source_pot[:, None, :, None]
         columns = jnp.where(live[:, :, None, None], columns, masked_score)

time: 748 us -> 716 us (0.957)
  blocking collectives: 564 us -> 531 us
    psum x3 -> x0, blocking collectives: 70.7 us -> none  [on_device(): total = lax.psum(local_sum, 'col')]
    all_gather x0 -> x3, blocking collectives: none -> 38.3 us  [on_device(): total = jnp.sum(lax.all_gather(local_sum, 'col'), axis=0)]
where the time goes in v1:
time: 716 us; the launch traced here: 715 us
  blocking collectives  531 us (74%)
  waiting for transfers between devices  71.4 us (10%)
  other arithmetic  54.6 us (8%)
  local copies, waits for them, and re-layouts  30 us (4%)
  between operations  14.3 us (2%)
  matrix products  13.5 us (2%)
    pmax x3, blocking collectives, on_device(): col_high = lax.pmax(local_top, 'row')  211 us
    psum x3, blocking collectives, on_device(): col_total = lax.psum(col_sum, 'row')  209 us
    pmax x3, blocking collectives, on_device(): highest = lax.pmax(row_top, 'col')  73.1 us
    all_gather x1, waiting for transfers between devices, on_device(): lax.all_gather(target_points, 'row', axis=1, tiled=True)  70.8 us
    all_gather x3, blocking collectives, on_device(): total = jnp.sum(lax.all_gather(local_sum, 'col'), axis=0)  38.3 us
    reduce_sum x3, other arithmetic, on_device(): sums = jnp.sum(jnp.exp(columns - slot_ref[:, :, None, :]), axis=2)  15.4 us
  transfers between devices with their start and end apart: 1, of which 1 were waited for; matrix products, arithmetic and copies ran while one was open for 1% of the time, Pallas kernels for 0%

profile of v1, /device:TPU:0, one launch (start us, length us, event | category | flops | bytes accessed | tf_op | source)
XLA Modules:
  0.0 715.2 jit_solution(16532274899149751317)
XLA Ops:
  7.9 0.8 copy.16
  8.7 0.7 compare_select_fusion
  10.2 0.7 log.24
  10.9 0.7 log.25
  11.6 0.7 iota_compare_fusion
  12.5 70.8 %all-gather.5.cloned.1.call-done = bf16[4096,1024]{0,1:T(8,128)(2,1)} async-done(((bf16[4096,64]{0,1:T(8,128)(2,1)}), bf16[4096,1024]{0,1:T(8,128)(2,1)}) %all-gather.5.cloned.1.call-update) | async-done | bytes 8388624 | tf_op jit(solution)/shard_map/all_gather | solution.py:34
  83.2 12.0 %copy.14 = bf16[4096,1024]{1,0:T(8,128)(2,1)} copy(bf16[4096,1024]{0,1:T(8,128)(2,1)} %all-gather.5.cloned.1.call-done) | data formatting | bytes 16777216 | tf_op jit(solution)/shard_map/all_gather | solution.py:34
  95.2 10.6 %gather_fusion = bf16[32,256,1024]{2,1,0:T(8,128)(2,1)} fusion(bf16[16,256,1024]{2,1,0:T(8,128)(2,1)} %bitcast.60, s32[1024]{0:T(1024)S(1)} %pad_clamp_fusion), kind=kCustom, calls=%fused_computation | custom fusion | bytes 33554560 | tf_op jit(solution)/shard_map/gather | solution.py:16
  105.8 13.5 %bitcast_reduce_fusion.5 = (f32[16,256]{1,0:T(8,128)S(1)}, f32[16,2,256,256]{3,2,1,0:T(8,128)}) fusion(f32[16,2,256]{2,1,0:T(2,128)S(1)} %reshape.108, pred[16,2]{1,0:T(8,128)(4,1)S(1)} %iota_compare_fusion, bf16[16,2,256,1024]{3,2,1,0:T(8,128)(2,1)} %bitcast.61, bf16[16,256,1024,1]{2,1,3,0:T(8,128)(2,1)} %bitcast.69), kind=kOutput, calls=%fused_computation.28 | convolution fusion | flops 4303351808 | bytes 33603616 | tf_op jit(solution)/shard_map/rad,rkbd->rkab/dot_general | solution.py:17
  119.3 25.8 %pmax.42 = f32[16,256]{1,0:T(8,128)S(1)} all-reduce(f32[16,256]{1,0:T(8,128)S(1)} %get-tuple-element.2), channel_id=1, replica_groups=mesh['row'=16,'col'=8] {'col'}, use_global_device_ids=true, to_apply=%region_1.2 | all-reduce | flops 4096 | bytes 32768 | tf_op jit(solution)/shard_map/pmax | solution.py:41
  145.1 4.7 fusion.11
  149.8 12.8 %all-gather = f32[128,256]{1,0:T(8,128)S(1)} all-gather(f32[16,256]{1,0:T(8,128)S(1)} %fusion.11), channel_id=2, replica_groups=mesh['row'=16,'col'=8] {'col'}, dimensions={0}, use_global_device_ids=true | all-gather | bytes 147456 | tf_op jit(solution)/shard_map/all_gather | solution.py:43
  162.6 4.7 bitcast_reduce_fusion.4
  167.4 72.4 %pmax.43 = f32[16,256]{1,0:T(8,128)S(1)} all-reduce(f32[16,256]{1,0:T(8,128)S(1)} %select_reduce_fusion.5), channel_id=1, replica_groups=mesh['row'=16,'col'=8] {'row'}, use_global_device_ids=true, to_apply=%region_6.7 | all-reduce | flops 4096 | bytes 32768 | tf_op jit(solution)/shard_map/pmax | solution.py:51
  240.4 5.1 fusion.9
  245.7 69.5 %psum.21 = f32[16,256]{1,0:T(8,128)S(1)} all-reduce(f32[16,256]{1,0:T(8,128)S(1)} %select_reduce_fusion.4), channel_id=1, replica_groups=mesh['row'=16,'col'=8] {'row'}, use_global_device_ids=true, to_apply=%region_9.10 | all-reduce | flops 4096 | bytes 32768 | tf_op jit(solution)/shard_map/psum | solution.py:55
  315.8 4.4 bitcast_reduce_fusion.3
  320.3 23.7 %pmax.44 = f32[16,256]{1,0:T(8,128)S(1)} all-reduce(f32[16,256]{1,0:T(8,128)S(1)} %bitcast_reduce_fusion.3), channel_id=1, replica_groups=mesh['row'=16,'col'=8] {'col'}, use_global_device_ids=true, to_apply=%region_11.12 | all-reduce | flops 4096 | bytes 32768 | tf_op jit(solution)/shard_map/pmax | solution.py:41
  344.0 4.6 fusion.7
  348.7 12.8 %all-gather.1 = f32[128,256]{1,0:T(8,128)S(1)} all-gather(f32[16,256]{1,0:T(8,128)S(1)} %fusion.7), channel_id=3, replica_groups=mesh['row'=16,'col'=8] {'col'}, dimensions={0}, use_global_device_ids=true | all-gather | bytes 147456 | tf_op jit(solution)/shard_map/all_gather | solution.py:43
  361.4 4.7 bitcast_reduce_fusion.2
  366.3 69.5 %pmax.45 = f32[16,256]{1,0:T(8,128)S(1)} all-reduce(f32[16,256]{1,0:T(8,128)S(1)} %select_reduce_fusion.3), channel_id=1, replica_groups=mesh['row'=16,'col'=8] {'row'}, use_global_device_ids=true, to_apply=%region_16.17 | all-reduce | flops 4096 | bytes 32768 | tf_op jit(solution)/shard_map/pmax | solution.py:51
  436.4 5.1 fusion.5
  441.7 69.5 %psum.22 = f32[16,256]{1,0:T(8,128)S(1)} all-reduce(f32[16,256]{1,0:T(8,128)S(1)} %select_reduce_fusion.2), channel_id=1, replica_groups=mesh['row'=16,'col'=8] {'row'}, use_global_device_ids=true, to_apply=%region_19.20 | all-reduce | flops 4096 | bytes 32768 | tf_op jit(solution)/shard_map/psum | solution.py:55
  511.9 4.4 bitcast_reduce_fusion.1
  516.3 23.6 %pmax.46 = f32[16,256]{1,0:T(8,128)S(1)} all-reduce(f32[16,256]{1,0:T(8,128)S(1)} %bitcast_reduce_fusion.1), channel_id=1, replica_groups=mesh['row'=16,'col'=8] {'col'}, use_global_device_ids=true, to_apply=%region_21.22 | all-reduce | flops 4096 | bytes 32768 | tf_op jit(solution)/shard_map/pmax | solution.py:41
  539.9 4.6 fusion.3
  544.5 12.8 %all-gather.2 = f32[128,256]{1,0:T(8,128)S(1)} all-gather(f32[16,256]{1,0:T(8,128)S(1)} %fusion.3), channel_id=4, replica_groups=mesh['row'=16,'col'=8] {'col'}, dimensions={0}, use_global_device_ids=true | all-gather | bytes 147456 | tf_op jit(solution)/shard_map/all_gather | solution.py:43
  557.3 4.7 bitcast_reduce_fusion
  562.1 69.5 %pmax.47 = f32[16,256]{1,0:T(8,128)S(1)} all-reduce(f32[16,256]{1,0:T(8,128)S(1)} %select_reduce_fusion.1), channel_id=1, replica_groups=mesh['row'=16,'col'=8] {'row'}, use_global_device_ids=true, to_apply=%region_26.27 | all-reduce | flops 4096 | bytes 32768 | tf_op jit(solution)/shard_map/pmax | solution.py:51
  632.3 5.1 fusion.1
  637.5 69.5 %psum.23 = f32[16,256]{1,0:T(8,128)S(1)} all-reduce(f32[16,256]{1,0:T(8,128)S(1)} %select_reduce_fusion), channel_id=1, replica_groups=mesh['row'=16,'col'=8] {'row'}, use_global_device_ids=true, to_apply=%region_29.30 | all-reduce | flops 4096 | bytes 32768 | tf_op jit(solution)/shard_map/psum | solution.py:55
  (38 shorter events, 6.9 us)
Async XLA Ops:
  7.2 76.1 %all-gather.5.cloned.1.call-start = ((), (), s32[]{:S(2)}) async-start(), calls=%async_computation | async-start | bytes 8912896 | tf_op jit(solution)/shard_map/all_gather | solution.py:34
Sparse Core Ops, SparseCore 0:
  10.1 73.0 all-gather.4
